TPU v7x, 512 devices: a whole 4x4x16 slice. The times are simulated.
512 devices in a mesh: rep: 32 (over x, y, z_hi), fsdp: 16 (over z_lo, core).
Axes of the slice: x: 4, y: 4, z: 16 (z_hi: 2, z_lo: 8; z = z_hi * 8 + z_lo), core: 2. Of those that a mesh axis runs over, the one named last changes fastest.
Arguments:
- activations: bfloat16 [65536, 8192], P(('rep', 'fsdp')), may hold values from -6 to 6
- key_grads: bfloat16 [65536, 512], P(('rep', 'fsdp')), may hold values from -6 to 6
- params: float32 [32, 8192, 512], P('rep', 'fsdp'), may hold values from -6 to 6
- first_moment: bfloat16 [32, 8192, 512], P('rep', 'fsdp'), may hold values from -4 to 4
- second_moment: bfloat16 [32, 8192, 512], P('rep', 'fsdp'), may hold values from 0.0099487305 to 1
- step_index: int32 [1], replicated, may hold values from 0 to 63
Outputs:
- key_out: bfloat16 [65536, 512], P(('rep', 'fsdp'))
- averaged: bfloat16 [32, 8192, 512], P('rep', 'fsdp')
All inputs are finite; a program needn't handle non-finite values.
Results may differ from a plain program's by a relative error of at most 0.0049.
Values may be sent and summed in bfloat16 or wider, within the bound.
A program may use at most 64 MiB of HBM per device.

v0:
```python
from functools import partial

import jax
import jax.numpy as jnp
from jax import lax
from jax.sharding import PartitionSpec as P

beta_one = 0.9
beta_two = 0.95
learn_rate = 0.25
epsilon = 1e-08


def swapped(value, axis, distance):
    mask = 2**distance
    pairs = [(source, source ^ mask) for source in range(lax.axis_size(axis))]
    return lax.ppermute(value, axis, pairs)


def adam_step(params, first_moment, second_moment, gradient, step_index):
    steps = (step_index[0] + 1).astype(jnp.float32)
    moment_one = beta_one * first_moment.astype(jnp.float32) + (1.0 - beta_one) * gradient
    moment_two = (
        beta_two * second_moment.astype(jnp.float32) + (1.0 - beta_two) * gradient * gradient
    )
    corr_one = 1.0 - jnp.power(jnp.float32(beta_one), steps)
    corr_two = 1.0 - jnp.power(jnp.float32(beta_two), steps)
    return params - learn_rate * (moment_one / corr_one) / (
        jnp.sqrt(moment_two / corr_two) + epsilon
    )


def from_partner(value, level):
    return swapped(value, "rep", level)


def per_device(activations, key_grads, params, first_moment, second_moment, step_index):
    factor = activations.shape[1] ** (-0.5)
    compute = params[0].astype(jnp.bfloat16)
    columns = lax.all_to_all(activations, "fsdp", split_axis=1, concat_axis=0, tiled=True)
    sliced = activations
    summed = jnp.dot(
        sliced,
        lax.all_gather(compute, "fsdp", axis=0, tiled=True),
        preferred_element_type=jnp.float32,
    )
    key_out = (summed * factor).astype(jnp.bfloat16)
    sliced = columns
    gradient = (
        lax.dot_general(
            sliced,
            lax.all_gather(key_grads, "fsdp", axis=0, tiled=True),
            (((0,), (0,)), ((), ())),
            preferred_element_type=jnp.float32,
        )
        * factor
    )
    updated = adam_step(params, first_moment, second_moment, gradient[None], step_index)
    levels = lax.axis_size("rep").bit_length() - 1
    which = step_index[0] % levels
    branches = [partial(from_partner, level=number) for number in range(levels)]
    other = lax.switch(which, branches, updated)
    averaged = (0.5 * (updated + other)).astype(jnp.bfloat16)
    return (key_out, averaged)


def solution(mesh):
    in_specs = (
        P(("rep", "fsdp"), None),
        P(("rep", "fsdp"), None),
        P("rep", "fsdp", None),
        P("rep", "fsdp", None),
        P("rep", "fsdp", None),
        P(),
    )
    out_specs = (P(("rep", "fsdp"), None), P("rep", "fsdp", None))
    return jax.shard_map(
        per_device, mesh=mesh, in_specs=in_specs, out_specs=out_specs, check_vma=False
    )
```

profile of v0, /device:TPU:1, one launch (start us, length us, event | category | flops | bytes accessed | tf_op | source)
XLA Modules:
  0.0 282.0 jit_solution(2881763253089359824)
XLA Ops:
  7.2 4.1 %copy.8 = bf16[128,8192]{0,1:T(8,128)(2,1)} copy(bf16[128,8192]{1,0:T(8,128)(2,1)} %param.11) | data formatting | bytes 4194304 | tf_op args[0]
  11.2 14.0 %all-to-all-start = ((bf16[128,16,512]{0,2,1:T(8,128)(2,1)}), bf16[128,16,512]{0,2,1:T(8,128)(2,1)S(1)}, u32[]{:S(2)}, u32[]{:S(2)}) async-start(bf16[128,16,512]{0,2,1:T(8,128)(2,1)} %bitcast.37), calls=%async_computation | async-start | bytes 4194304 | tf_op jit(solution)/shard_map/all_to_all | solution.py:40
  25.3 0.0 all-gather.4.cloned.1.call-start
  25.3 0.7 all-gather.4.cloned.1.call-update
  26.0 0.0 all-gather.6.cloned.1.call-start
  26.8 91.4 %all-to-all-done = bf16[128,16,512]{0,2,1:T(8,128)(2,1)S(1)} async-done(((bf16[128,16,512]{0,2,1:T(8,128)(2,1)}), bf16[128,16,512]{0,2,1:T(8,128)(2,1)S(1)}, u32[]{:S(2)}, u32[]{:S(2)}) %all-to-all-start) | async-done | bytes 2097184 | tf_op jit(solution)/shard_map/all_to_all | solution.py:40
  118.2 2.6 copy.9
  120.8 28.3 %all-gather.4.cloned.1.call-done = bf16[2048,512]{1,0:T(8,128)(2,1)} async-done(((bf16[128,512]{1,0:T(8,128)(2,1)}), bf16[2048,512]{1,0:T(8,128)(2,1)}) %all-gather.4.cloned.1.call-update) | async-done | bytes 2097168 | tf_op jit(solution)/shard_map/all_gather | solution.py:52
  149.2 5.8 %fusion.12 = (f32[1,512,512]{2,1,0:T(8,128)S(1)}, bf16[1,512,512]{2,1,0:T(8,128)(2,1)}) fusion(f32[1,512,512]{2,1,0:T(8,128)} %param.13, bf16[1,512,512]{2,1,0:T(8,128)(2,1)} %param.15, bf16[1,512,512]{2,1,0:T(8,128)(2,1)} %param.14, f32[]{:T(128)} %bitcast.7, f32[]{:T(128)} %bitcast.5, bf16[2048,512]{1,0:T(8,128)(2,1)} %bitcast.38, ...), kind=kOutput, calls=%fused_computation.9 | convolution fusion | flops 1078198272 | bytes 7864328 | tf_op jit(solution)/shard_map/dot_general | solution.py:50
  155.0 0.0 copy-start
  155.0 0.0 all-gather.6.cloned.1.call-update
  155.1 23.2 %conditional.1 = (f32[1,512,512]{2,1,0:T(8,128)}) conditional(s32[]{:T(128)} %clamp.3, f32[1,512,512]{2,1,0:T(8,128)S(1)} %get-tuple-element.13, f32[1,512,512]{2,1,0:T(8,128)S(1)} %get-tuple-element.13, f32[1,512,512]{2,1,0:T(8,128)S(1)} %get-tuple-element.13, f32[1,512,512]{2,1,0:T(8,128)S(1)} %get-tuple-element.13, ...), branch_computations={%region_0.1_spmd, %region_1.2_spmd, %region_2.3_spmd, %region_3.4_... | conditional | bytes 4194352 | solution.py:62
  155.1 3.7 %collective-permute-start.3 = (f32[1,512,512]{2,1,0:T(8,128)S(1)}, f32[1,512,512]{2,1,0:T(8,128)}, u32[]{:S(2)}, u32[]{:S(2)}) collective-permute-start(f32[1,512,512]{2,1,0:T(8,128)S(1)} %param.3), channel_id=1, source_target_pairs={{0,128},{16,144},{32,160},{48,176},{64,192},{80,208},{96,224},{112... | collective-permute-start | bytes 3145736 | tf_op jit(solution)/shard_map/cond/branch_3_fun/ppermute | solution.py:17
  158.8 19.4 %collective-permute-done.3 = f32[1,512,512]{2,1,0:T(8,128)} collective-permute-done((f32[1,512,512]{2,1,0:T(8,128)S(1)}, f32[1,512,512]{2,1,0:T(8,128)}, u32[]{:S(2)}, u32[]{:S(2)}) %collective-permute-start.3) | collective-permute-done | bytes 1048608 | tf_op jit(solution)/shard_map/cond/branch_3_fun/ppermute | solution.py:17
  178.2 2.3 multiply_convert_fusion
  180.5 89.4 %all-gather.6.cloned.1.call-done = bf16[1,8192,512]{2,1,0:T(8,128)(2,1)} async-done(((bf16[1,512,512]{2,1,0:T(8,128)(2,1)}), bf16[1,8192,512]{2,1,0:T(8,128)(2,1)}) %all-gather.6.cloned.1.call-update) | async-done | bytes 8388624 | tf_op jit(solution)/shard_map/all_gather | solution.py:44
  269.8 0.0 copy-done
  269.9 5.3 %fusion.5 = bf16[128,512]{1,0:T(8,128)(2,1)} fusion(bf16[128,8192]{1,0:T(8,128)(2,1)S(1)} %copy-done, bf16[1,8192,512]{2,1,0:T(8,128)(2,1)} %all-gather.6.cloned.1.call-done), kind=kOutput, calls=%fused_computation.3 | convolution fusion | flops 1073872896 | bytes 10616832 | tf_op jit(solution)/shard_map/dot_general | solution.py:42
Async XLA Ops:
  11.2 107.0 %all-to-all-start = ((bf16[128,16,512]{0,2,1:T(8,128)(2,1)}), bf16[128,16,512]{0,2,1:T(8,128)(2,1)S(1)}, u32[]{:S(2)}, u32[]{:S(2)}) async-start(bf16[128,16,512]{0,2,1:T(8,128)(2,1)} %bitcast.37), calls=%async_computation | async-start | bytes 4194304 | tf_op jit(solution)/shard_map/all_to_all | solution.py:40
  25.3 123.9 %all-gather.4.cloned.1.call-start = ((), (), s32[]{:S(2)}) async-start(), calls=%async_computation.1 | async-start | bytes 2228224 | tf_op jit(solution)/shard_map/all_gather | solution.py:52
  26.0 243.8 %all-gather.6.cloned.1.call-start = ((), (), s32[]{:S(2)}) async-start(), calls=%async_computation.2 | async-start | bytes 8912896 | tf_op jit(solution)/shard_map/all_gather | solution.py:44
  155.0 114.8 %copy-start = (bf16[128,8192]{1,0:T(8,128)(2,1)S(1)}, bf16[128,8192]{1,0:T(8,128)(2,1)}, u32[]{:S(2)}) copy-start(bf16[128,8192]{1,0:T(8,128)(2,1)} %param.11) | copy-start | bytes 6291460
  155.1 23.1 %collective-permute-start.3 = (f32[1,512,512]{2,1,0:T(8,128)S(1)}, f32[1,512,512]{2,1,0:T(8,128)}, u32[]{:S(2)}, u32[]{:S(2)}) collective-permute-start(f32[1,512,512]{2,1,0:T(8,128)S(1)} %param.3), channel_id=1, source_target_pairs={{0,128},{16,144},{32,160},{48,176},{64,192},{80,208},{96,224},{112... | collective-permute-start | bytes 3145736 | tf_op jit(solution)/shard_map/cond/branch_3_fun/ppermute | solution.py:17
Sparse Core Ops, SparseCore 0:
  28.2 120.9 all-gather.3
  155.2 114.6 all-gather.5
where the time goes:
time: 286 us; the launch traced here: 282 us
  waiting for transfers between devices  229 us (80%)
  starting transfers between devices  17.8 us (6%)
  between operations  14.8 us (5%)
  matrix products  11.1 us (4%)
  local copies, waits for them, and re-layouts  6.67 us (2%)
    all_to_all x1, waiting for transfers between devices, per_device(): lax.all_to_all(activations, 'fsdp', split_axis=1, concat_axis=0, tiled=True)  91.4 us
    all_gather x1, waiting for transfers between devices, per_device(): lax.all_gather(compute, 'fsdp', axis=0, tiled=True)  89.4 us
    all_gather x1, waiting for transfers between devices, per_device(): lax.all_gather(key_grads, 'fsdp', axis=0, tiled=True)  28.3 us
    ppermute x1, waiting for transfers between devices, swapped(): return lax.ppermute(value, axis, pairs)  19.4 us
    all_to_all x1, starting transfers between devices, per_device(): lax.all_to_all(activations, 'fsdp', split_axis=1, concat_axis=0, tiled=True)  14 us
    dot_general x1, matrix products, per_device(): lax.dot_general(sliced, lax.all_gather(key_grads, 'fsdp', axis=0, tiled=T...  5.85 us
  transfers between devices with their start and end apart: 4, of which 4 were waited for; matrix products, arithmetic and copies ran while one was open for 2% of the time, Pallas kernels for 0%

commit v1 on v0

v1 whole, which is shorter than its diff:
```python
import functools
import math

import jax
import jax.numpy as jnp
from jax import lax
from jax.experimental import pallas as pl
from jax.experimental.pallas import tpu as pltpu
from jax.sharding import PartitionSpec as P

MESH = pl.DeviceIdType.MESH
beta_one = 0.9
beta_two = 0.95
learn_rate = 0.25
epsilon = 1e-08
PIECES = 4


def step_kernel(
    level, chips, factor, pieces,
    x, g, p, m, v, t,
    key_out, averaged,
    xl, xc, gc, par, mom, var, wall, acc, new, mine, theirs, ksum, kout, aout,
    lsem, xsend, xrecv, gsend, grecv, usend, urecv, dsend, drecv, bsend, brecv, psend, precv, osem,
):
    rep, me = lax.axis_index("rep"), lax.axis_index("fsdp")
    z = me // 2
    core = me - 2 * z
    last = chips - 1
    sib = me + 1 - 2 * core
    mask = 2**level
    mate = rep + mask * (1 - 2 * ((rep // mask) % 2))
    tokens, rows = g.shape[0], p.shape[1]
    piece = rows // pieces
    not_top, not_bottom = z < last, z > 0

    def block(index):
        return pl.ds(pl.multiple_of(index * rows, rows), rows)

    def part(s):
        return pl.ds(pl.multiple_of(s * piece, piece), piece)

    load_p = pltpu.make_async_copy(p.at[0], par, lsem.at[0])
    load_p.start()
    load_x = pltpu.make_async_copy(x, xl, lsem.at[1])
    load_x.start()
    load_g = pltpu.make_async_copy(g, gc.at[pl.ds(0, tokens)], lsem.at[2])
    load_g.start()
    for d in range(chips):
        pltpu.make_async_copy(
            x.at[:, block(2 * d + core)], xc.at[d, pl.ds(0, tokens)], lsem.at[3]
        ).start()
    load_m = pltpu.make_async_copy(m.at[0], mom, lsem.at[4])
    load_m.start()
    load_v = pltpu.make_async_copy(v.at[0], var, lsem.at[5])
    load_v.start()

    barrier = pltpu.get_barrier_semaphore()

    @pl.when(not_top)
    def _():
        pl.semaphore_signal(barrier, inc=1, device_id=(rep, me + 2), device_id_type=MESH)

    @pl.when(not_bottom)
    def _():
        pl.semaphore_signal(barrier, inc=1, device_id=(rep, me - 2), device_id_type=MESH)

    pl.semaphore_signal(barrier, inc=1, device_id=(rep, sib), device_id_type=MESH)
    pl.semaphore_signal(barrier, inc=1, device_id=(mate, me), device_id_type=MESH)
    load_p.wait()
    wall[me] = par[...].astype(jnp.bfloat16)
    pl.semaphore_wait(barrier, 2 + not_top.astype(jnp.int32) + not_bottom.astype(jnp.int32))

    def up(ref, k, s):
        return pltpu.make_async_remote_copy(
            src_ref=ref, dst_ref=ref, send_sem=usend.at[k * pieces + s], recv_sem=urecv.at[k * pieces + s],
            device_id=(rep, me + 2), device_id_type=MESH,
        )

    def down(ref, k, s):
        return pltpu.make_async_remote_copy(
            src_ref=ref, dst_ref=ref, send_sem=dsend.at[k * pieces + s], recv_sem=drecv.at[k * pieces + s],
            device_id=(rep, me - 2), device_id_type=MESH,
        )

    def beside(chip):
        ref = wall.at[2 * chip + core]
        return pltpu.make_async_remote_copy(
            src_ref=ref, dst_ref=ref, send_sem=bsend.at[chip], recv_sem=brecv.at[chip],
            device_id=(rep, sib), device_id_type=MESH,
        )

    def from_beside(chip):
        ref = wall.at[2 * chip + 1 - core]
        return pltpu.make_async_remote_copy(
            src_ref=ref, dst_ref=ref, send_sem=bsend.at[chip], recv_sem=brecv.at[chip],
            device_id=(rep, sib), device_id_type=MESH,
        )

    def to_mate(s):
        return pltpu.make_async_remote_copy(
            src_ref=mine.at[part(s)], dst_ref=theirs.at[part(s)], send_sem=psend.at[s], recv_sem=precv.at[s],
            device_id=(mate, me), device_id_type=MESH,
        )

    for s in range(pieces):

        @pl.when(not_top)
        def _(s=s):
            up(wall.at[me, part(s)], 0, s).start()

        @pl.when(not_bottom)
        def _(s=s):
            down(wall.at[me, part(s)], 0, s).start()

    swap_g = pltpu.make_async_remote_copy(
        src_ref=g, dst_ref=gc.at[pl.ds(tokens, tokens)], send_sem=gsend, recv_sem=grecv,
        device_id=(rep, sib), device_id_type=MESH,
    )
    swap_g.start()
    for d in range(chips):
        pltpu.make_async_remote_copy(
            src_ref=x.at[:, block(2 * d + 1 - core)], dst_ref=xc.at[d, pl.ds(tokens, tokens)],
            send_sem=xsend, recv_sem=xrecv, device_id=(rep, sib), device_id_type=MESH,
        ).start()
    beside(z).start()
    load_x.wait()
    load_g.wait()
    load_m.wait()
    load_v.wait()
    whole = pltpu.make_async_remote_copy(
        src_ref=xc.at[:, pl.ds(0, tokens)], dst_ref=xc.at[:, pl.ds(tokens, tokens)],
        send_sem=xsend, recv_sem=xrecv, device_id=(rep, sib), device_id_type=MESH,
    )
    pltpu.make_async_copy(
        xc.at[:, pl.ds(0, tokens)], xc.at[:, pl.ds(0, tokens)], lsem.at[3]
    ).wait()
    whole.wait()
    swap_g.wait()

    def project(index):
        ksum[...] += jnp.dot(xl[:, block(index)], wall[index], preferred_element_type=jnp.float32)

    ksum[...] = jnp.dot(xl[:, block(me)], wall[me], preferred_element_type=jnp.float32)

    def partial(d, s):
        return lax.dot_general(
            xc[d, :, part(s)], gc[...], (((0,), (0,)), ((), ())), preferred_element_type=jnp.float32
        )

    def add_to(slot, d, s, received):
        own = partial(d, s)

        @pl.when(received)
        def _():
            acc[slot, part(s), :] = (own + acc[slot, part(s), :].astype(jnp.float32)).astype(jnp.bfloat16)

        @pl.when(jnp.logical_not(received))
        def _():
            acc[slot, part(s), :] = own.astype(jnp.bfloat16)

    def turn(i, carry):
        k, s = i // pieces, i % pieces

        @pl.when(k <= z)
        def _():
            chip = z - k
            ref = wall.at[2 * chip + core, part(s)]
            up(ref, k - 1, s).wait_recv()

            @pl.when(not_top)
            def _():
                up(ref, k, s).start()

        @pl.when(k <= last - z)
        def _():
            chip = z + k
            ref = wall.at[2 * chip + core, part(s)]
            down(ref, k - 1, s).wait_recv()

            @pl.when(not_bottom)
            def _():
                down(ref, k, s).start()

        @pl.when(k > z)
        def _():
            d = chips + z - k
            ref = acc.at[d + 1, part(s)]

            @pl.when(not_bottom)
            def _():
                up(ref, k - 1, s).wait_recv()

            add_to(d + 1, d, s, not_bottom)
            up(ref, k, s).start()

        @pl.when(k > last - z)
        def _():
            d = z + k - chips
            ref = acc.at[d, part(s)]

            @pl.when(not_top)
            def _():
                down(ref, k - 1, s).wait_recv()

            add_to(d, d, s, not_top)
            down(ref, k, s).start()

        @pl.when(s == pieces - 1)
        def _():
            @pl.when(k <= z)
            def _():
                beside(z - k).start()
                project(2 * (z - k) + core)

            @pl.when(k <= last - z)
            def _():
                beside(z + k).start()
                project(2 * (z + k) + core)

            @pl.when(k - 1 <= z)
            def _():
                from_beside(z - k + 1).wait_recv()
                project(2 * (z - k + 1) + 1 - core)

            @pl.when(jnp.logical_and(k > 1, k - 1 <= last - z))
            def _():
                from_beside(z + k - 1).wait_recv()
                project(2 * (z + k - 1) + 1 - core)

        return carry

    lax.fori_loop(pieces, chips * pieces, turn, 0)

    @pl.when(z == last)
    def _():
        from_beside(0).wait_recv()
        project(1 - core)

    @pl.when(z == 0)
    def _():
        from_beside(last).wait_recv()
        project(2 * last + 1 - core)

    kout[...] = (ksum[...] * factor).astype(jnp.bfloat16)
    store_k = pltpu.make_async_copy(kout, key_out, osem.at[pieces])
    store_k.start()

    steps = jnp.full((1, g.shape[1]), t[0] + 1, jnp.int32).astype(jnp.float32)
    corr_one = 1.0 - jnp.exp(steps * math.log(beta_one))
    corr_two = 1.0 - jnp.exp(steps * math.log(beta_two))

    def finish(s, carry):
        new[part(s), :] = partial(z, s)

        @pl.when(not_bottom)
        def _():
            up(acc.at[z + 1, part(s)], last, s).wait_recv()
            new[part(s), :] += acc[z + 1, part(s), :].astype(jnp.float32)

        @pl.when(not_top)
        def _():
            down(acc.at[z, part(s)], last, s).wait_recv()
            new[part(s), :] += acc[z, part(s), :].astype(jnp.float32)

        gradient = new[part(s), :] * factor
        one = beta_one * mom[part(s), :].astype(jnp.float32) + (1.0 - beta_one) * gradient
        two = beta_two * var[part(s), :].astype(jnp.float32) + (1.0 - beta_two) * gradient * gradient
        updated = par[part(s), :] - learn_rate * (one / corr_one) / (jnp.sqrt(two / corr_two) + epsilon)
        new[part(s), :] = updated
        mine[part(s), :] = updated.astype(jnp.bfloat16)
        to_mate(s).start()
        return carry

    lax.fori_loop(0, pieces, finish, 0)

    def store_a(s):
        return pltpu.make_async_copy(aout.at[part(s)], averaged.at[0, part(s)], osem.at[s])

    def average(s, carry):
        to_mate(s).wait_recv()
        aout[part(s), :] = (0.5 * (new[part(s), :] + theirs[part(s), :].astype(jnp.float32))).astype(jnp.bfloat16)
        store_a(s).start()
        return carry

    lax.fori_loop(0, pieces, average, 0)

    def sent(i, carry):
        k, s = i // pieces, i % pieces

        @pl.when(not_top)
        def _():
            up(acc.at[0, part(s)], k, s).wait_send()

        @pl.when(not_bottom)
        def _():
            down(acc.at[0, part(s)], k, s).wait_send()

        return carry

    lax.fori_loop(0, chips * pieces, sent, 0)
    for chip in range(chips):
        beside(chip).wait_send()
    for s in range(pieces):
        to_mate(s).wait_send()
        store_a(s).wait()
    store_k.wait()


def call(level, chips, factor, x, g, p, m, v, t):
    tokens, width = g.shape
    rows = p.shape[1]
    pieces = PIECES
    dma = pltpu.SemaphoreType.DMA
    any_space = pl.BlockSpec(memory_space=pl.ANY)
    return pl.pallas_call(
        functools.partial(step_kernel, level, chips, factor, pieces),
        out_shape=(
            jax.ShapeDtypeStruct((tokens, width), jnp.bfloat16),
            jax.ShapeDtypeStruct((1, rows, width), jnp.bfloat16),
        ),
        in_specs=[any_space] * 5 + [pl.BlockSpec(memory_space=pltpu.SMEM)],
        out_specs=(any_space, any_space),
        scratch_shapes=[
            pltpu.VMEM(x.shape, jnp.bfloat16),
            pltpu.VMEM((chips, 2 * tokens, rows), jnp.bfloat16),
            pltpu.VMEM((2 * tokens, width), jnp.bfloat16),
            pltpu.VMEM((rows, width), jnp.float32),
            pltpu.VMEM((rows, width), jnp.bfloat16),
            pltpu.VMEM((rows, width), jnp.bfloat16),
            pltpu.VMEM((2 * chips, rows, width), jnp.bfloat16),
            pltpu.VMEM((chips + 1, rows, width), jnp.bfloat16),
            pltpu.VMEM((rows, width), jnp.float32),
            pltpu.VMEM((rows, width), jnp.bfloat16),
            pltpu.VMEM((rows, width), jnp.bfloat16),
            pltpu.VMEM((tokens, width), jnp.float32),
            pltpu.VMEM((tokens, width), jnp.bfloat16),
            pltpu.VMEM((rows, width), jnp.bfloat16),
            dma((6,)),
            dma, dma, dma, dma,
            dma((chips * pieces,)), dma((chips * pieces,)),
            dma((chips * pieces,)), dma((chips * pieces,)),
            dma((chips,)), dma((chips,)),
            dma((pieces,)), dma((pieces,)),
            dma((pieces + 1,)),
        ],
        compiler_params=pltpu.CompilerParams(
            collective_id=level, has_side_effects=True, vmem_limit_bytes=48 * 2**20
        ),
        cost_estimate=pl.CostEstimate(
            flops=4 * tokens * width * x.shape[1], bytes_accessed=6 * 2**20, transcendentals=0
        ),
        name=f"level_{level}",
    )(x, g, p, m, v, t)


def per_device(activations, key_grads, params, first_moment, second_moment, step_index):
    factor = activations.shape[1] ** (-0.5)
    chips = lax.axis_size("fsdp") // 2
    levels = lax.axis_size("rep").bit_length() - 1
    branches = [functools.partial(call, level, chips, factor) for level in range(levels)]
    return lax.switch(
        step_index[0] % levels, branches, activations, key_grads, params, first_moment, second_moment, step_index
    )


def solution(mesh):
    in_specs = (
        P(("rep", "fsdp"), None),
        P(("rep", "fsdp"), None),
        P("rep", "fsdp", None),
        P("rep", "fsdp", None),
        P("rep", "fsdp", None),
        P(),
    )
    out_specs = (P(("rep", "fsdp"), None), P("rep", "fsdp", None))
    return jax.shard_map(
        per_device, mesh=mesh, in_specs=in_specs, out_specs=out_specs, check_vma=False
    )
```

time: 286 us -> 154 us (0.54)
  the two profiles are of different devices: /device:TPU:1 before, /device:TPU:22 now
where the time goes in v1:
time: 154 us
  Pallas kernels  151 us (98%)
    pallas_call x1, Pallas kernels, call(): pl.pallas_call(functools.partial(step_kernel, level, chips, factor, piece...  151 us

profile of v1, /device:TPU:22, one launch (start us, length us, event | category | flops | bytes accessed | tf_op | source)
XLA Modules:
  0.0 154.3 jit_solution(3053244248845722967)
XLA Ops:
  1.3 151.5 %conditional.1 = ((bf16[128,512]{1,0:T(8,128)(2,1)S(1)}, bf16[1,512,512]{2,1,0:T(8,128)(2,1)S(1)})) conditional(s32[]{:T(128)} %clamp.3, (bf16[128,8192]{1,0:T(8,128)(2,1)}, bf16[128,512]{1,0:T(8,128)(2,1)}, f32[1,512,512]{2,1,0:T(8,128)}, bf16[1,512,512]{2,1,0:T(8,128)(2,1)}, bf16[1,512,512]{2,1,0:T(8,128)(2,1)}, ...), branch_computations={%region_0.1_spmd, %region_1.2_spmd, %region_2.3_spmd, %region_3.4_... | conditional | flops 2147483648 | bytes 6291464 | solution.py:362
  1.3 151.5 %level_0.1 = (bf16[128,512]{1,0:T(8,128)(2,1)S(1)}, bf16[1,512,512]{2,1,0:T(8,128)(2,1)S(1)}) custom-call(bf16[128,8192]{1,0:T(8,128)(2,1)} %get-tuple-element.60.x, bf16[128,512]{1,0:T(8,128)(2,1)} %get-tuple-element.61.g, f32[1,512,512]{2,1,0:T(8,128)} %get-tuple-element.62.p, bf16[1,512,512]{2,1,0:T(8,128)(2,1)} %get-tuple-element.63.m, ...), custom_call_target="tpu_custom_call" | custom-call | flops 2147483648 | bytes 6291456 | tf_op jit(solution)/shard_map/cond/branch_0_fun/level_0/pallas_call | solution.py:316
  152.8 0.7 copy.31
  153.5 0.8 copy.32

commit v2 on v1

--- a/solution.py
+++ b/solution.py
@@ -13,15 +13,16 @@
 beta_two = 0.95
 learn_rate = 0.25
 epsilon = 1e-08
-PIECES = 4
+PIECES = 2
+TAIL = 8
 
 
 def step_kernel(
-    level, chips, factor, pieces,
+    level, chips, factor, pieces, tail,
     x, g, p, m, v, t,
     key_out, averaged,
     xl, xc, gc, par, mom, var, wall, acc, new, mine, theirs, ksum, kout, aout,
-    lsem, xsend, xrecv, gsend, grecv, usend, urecv, dsend, drecv, bsend, brecv, psend, precv, osem,
+    fsem, lsem, xsend, xrecv, gsend, grecv, usend, urecv, dsend, drecv, bsend, brecv, psend, precv, osem,
 ):
     rep, me = lax.axis_index("rep"), lax.axis_index("fsdp")
     z = me // 2
@@ -31,7 +32,8 @@
     mask = 2**level
     mate = rep + mask * (1 - 2 * ((rep // mask) % 2))
     tokens, rows = g.shape[0], p.shape[1]
-    piece = rows // pieces
+    piece, small = rows // pieces, rows // tail
+    split = tail // pieces
     not_top, not_bottom = z < last, z > 0
 
     def block(index):
@@ -40,8 +42,25 @@
     def part(s):
         return pl.ds(pl.multiple_of(s * piece, piece), piece)
 
-    load_p = pltpu.make_async_copy(p.at[0], par, lsem.at[0])
-    load_p.start()
+    def bit(j):
+        return pl.ds(pl.multiple_of(j * small, small), small)
+
+    barrier = pltpu.get_barrier_semaphore()
+
+    @pl.when(not_top)
+    def _():
+        pl.semaphore_signal(barrier, inc=1, device_id=(rep, me + 2), device_id_type=MESH)
+
+    @pl.when(not_bottom)
+    def _():
+        pl.semaphore_signal(barrier, inc=1, device_id=(rep, me - 2), device_id_type=MESH)
+
+    pl.semaphore_signal(barrier, inc=1, device_id=(rep, sib), device_id_type=MESH)
+    pl.semaphore_signal(barrier, inc=1, device_id=(mate, me), device_id_type=MESH)
+
+    load_p = [pltpu.make_async_copy(p.at[0, part(s)], par.at[part(s)], fsem.at[s]) for s in range(pieces)]
+    for s in range(pieces):
+        load_p[s].start()
     load_x = pltpu.make_async_copy(x, xl, lsem.at[1])
     load_x.start()
     load_g = pltpu.make_async_copy(g, gc.at[pl.ds(0, tokens)], lsem.at[2])
@@ -55,22 +74,6 @@
     load_v = pltpu.make_async_copy(v.at[0], var, lsem.at[5])
     load_v.start()
 
-    barrier = pltpu.get_barrier_semaphore()
-
-    @pl.when(not_top)
-    def _():
-        pl.semaphore_signal(barrier, inc=1, device_id=(rep, me + 2), device_id_type=MESH)
-
-    @pl.when(not_bottom)
-    def _():
-        pl.semaphore_signal(barrier, inc=1, device_id=(rep, me - 2), device_id_type=MESH)
-
-    pl.semaphore_signal(barrier, inc=1, device_id=(rep, sib), device_id_type=MESH)
-    pl.semaphore_signal(barrier, inc=1, device_id=(mate, me), device_id_type=MESH)
-    load_p.wait()
-    wall[me] = par[...].astype(jnp.bfloat16)
-    pl.semaphore_wait(barrier, 2 + not_top.astype(jnp.int32) + not_bottom.astype(jnp.int32))
-
     def up(ref, k, s):
         return pltpu.make_async_remote_copy(
             src_ref=ref, dst_ref=ref, send_sem=usend.at[k * pieces + s], recv_sem=urecv.at[k * pieces + s],
@@ -83,6 +86,34 @@
             device_id=(rep, me - 2), device_id_type=MESH,
         )
 
+    def up_last(j):
+        ref = acc.at[z + 2, bit(j)]
+        return pltpu.make_async_remote_copy(
+            src_ref=ref, dst_ref=ref, send_sem=usend.at[last * pieces + j], recv_sem=urecv.at[last * pieces + j],
+            device_id=(rep, me + 2), device_id_type=MESH,
+        )
+
+    def down_last(j):
+        ref = acc.at[z - 1, bit(j)]
+        return pltpu.make_async_remote_copy(
+            src_ref=ref, dst_ref=ref, send_sem=dsend.at[last * pieces + j], recv_sem=drecv.at[last * pieces + j],
+            device_id=(rep, me - 2), device_id_type=MESH,
+        )
+
+    def up_from(j):
+        ref = acc.at[z + 1, bit(j)]
+        return pltpu.make_async_remote_copy(
+            src_ref=ref, dst_ref=ref, send_sem=usend.at[last * pieces + j], recv_sem=urecv.at[last * pieces + j],
+            device_id=(rep, me - 2), device_id_type=MESH,
+        )
+
+    def down_from(j):
+        ref = acc.at[z, bit(j)]
+        return pltpu.make_async_remote_copy(
+            src_ref=ref, dst_ref=ref, send_sem=dsend.at[last * pieces + j], recv_sem=drecv.at[last * pieces + j],
+            device_id=(rep, me + 2), device_id_type=MESH,
+        )
+
     def beside(chip):
         ref = wall.at[2 * chip + core]
         return pltpu.make_async_remote_copy(
@@ -99,11 +130,15 @@
 
     def to_mate(s):
         return pltpu.make_async_remote_copy(
-            src_ref=mine.at[part(s)], dst_ref=theirs.at[part(s)], send_sem=psend.at[s], recv_sem=precv.at[s],
+            src_ref=mine.at[bit(s)], dst_ref=theirs.at[bit(s)], send_sem=psend.at[s], recv_sem=precv.at[s],
             device_id=(mate, me), device_id_type=MESH,
         )
 
     for s in range(pieces):
+        load_p[s].wait()
+        wall[me, part(s)] = par[part(s), :].astype(jnp.bfloat16)
+        if s == 0:
+            pl.semaphore_wait(barrier, 2 + not_top.astype(jnp.int32) + not_bottom.astype(jnp.int32))
 
         @pl.when(not_top)
         def _(s=s):
@@ -192,7 +227,15 @@
                 up(ref, k - 1, s).wait_recv()
 
             add_to(d + 1, d, s, not_bottom)
-            up(ref, k, s).start()
+
+            @pl.when(k < last)
+            def _():
+                up(ref, k, s).start()
+
+            @pl.when(k == last)
+            def _():
+                for q in range(split):
+                    up_last(s * split + q).start()
 
         @pl.when(k > last - z)
         def _():
@@ -204,7 +247,15 @@
                 down(ref, k - 1, s).wait_recv()
 
             add_to(d, d, s, not_top)
-            down(ref, k, s).start()
+
+            @pl.when(k < last)
+            def _():
+                down(ref, k, s).start()
+
+            @pl.when(k == last)
+            def _():
+                for q in range(split):
+                    down_last(s * split + q).start()
 
         @pl.when(s == pieces - 1)
         def _():
@@ -231,6 +282,12 @@
         return carry
 
     lax.fori_loop(pieces, chips * pieces, turn, 0)
+
+    def own_term(s, carry):
+        new[part(s), :] = partial(z, s)
+        return carry
+
+    lax.fori_loop(0, pieces, own_term, 0)
 
     @pl.when(z == last)
     def _():
@@ -243,47 +300,48 @@
         project(2 * last + 1 - core)
 
     kout[...] = (ksum[...] * factor).astype(jnp.bfloat16)
-    store_k = pltpu.make_async_copy(kout, key_out, osem.at[pieces])
+    store_k = pltpu.make_async_copy(kout, key_out, osem.at[tail])
     store_k.start()
 
     steps = jnp.full((1, g.shape[1]), t[0] + 1, jnp.int32).astype(jnp.float32)
     corr_one = 1.0 - jnp.exp(steps * math.log(beta_one))
     corr_two = 1.0 - jnp.exp(steps * math.log(beta_two))
 
-    def finish(s, carry):
-        new[part(s), :] = partial(z, s)
+    def finish(j, carry):
+        at = bit(j)
+        own = new[at, :]
 
         @pl.when(not_bottom)
         def _():
-            up(acc.at[z + 1, part(s)], last, s).wait_recv()
-            new[part(s), :] += acc[z + 1, part(s), :].astype(jnp.float32)
+            up_from(j).wait_recv()
 
         @pl.when(not_top)
         def _():
-            down(acc.at[z, part(s)], last, s).wait_recv()
-            new[part(s), :] += acc[z, part(s), :].astype(jnp.float32)
-
-        gradient = new[part(s), :] * factor
-        one = beta_one * mom[part(s), :].astype(jnp.float32) + (1.0 - beta_one) * gradient
-        two = beta_two * var[part(s), :].astype(jnp.float32) + (1.0 - beta_two) * gradient * gradient
-        updated = par[part(s), :] - learn_rate * (one / corr_one) / (jnp.sqrt(two / corr_two) + epsilon)
-        new[part(s), :] = updated
-        mine[part(s), :] = updated.astype(jnp.bfloat16)
-        to_mate(s).start()
-        return carry
-
-    lax.fori_loop(0, pieces, finish, 0)
-
-    def store_a(s):
-        return pltpu.make_async_copy(aout.at[part(s)], averaged.at[0, part(s)], osem.at[s])
-
-    def average(s, carry):
-        to_mate(s).wait_recv()
-        aout[part(s), :] = (0.5 * (new[part(s), :] + theirs[part(s), :].astype(jnp.float32))).astype(jnp.bfloat16)
-        store_a(s).start()
-        return carry
-
-    lax.fori_loop(0, pieces, average, 0)
+            down_from(j).wait_recv()
+
+        below = jnp.where(not_bottom, acc[z + 1, at, :].astype(jnp.float32), 0.0)
+        above = jnp.where(not_top, acc[z, at, :].astype(jnp.float32), 0.0)
+        gradient = (own + below + above) * factor
+        one = beta_one * mom[at, :].astype(jnp.float32) + (1.0 - beta_one) * gradient
+        two = beta_two * var[at, :].astype(jnp.float32) + (1.0 - beta_two) * gradient * gradient
+        updated = par[at, :] - learn_rate * (one / corr_one) / (jnp.sqrt(two / corr_two) + epsilon)
+        new[at, :] = updated
+        mine[at, :] = updated.astype(jnp.bfloat16)
+        to_mate(j).start()
+        return carry
+
+    lax.fori_loop(0, tail, finish, 0)
+
+    def store_a(j):
+        return pltpu.make_async_copy(aout.at[bit(j)], averaged.at[0, bit(j)], osem.at[j])
+
+    def average(j, carry):
+        to_mate(j).wait_recv()
+        aout[bit(j), :] = (0.5 * (new[bit(j), :] + theirs[bit(j), :].astype(jnp.float32))).astype(jnp.bfloat16)
+        store_a(j).start()
+        return carry
+
+    lax.fori_loop(0, tail, average, 0)
 
     def sent(i, carry):
         k, s = i // pieces, i % pieces
@@ -298,23 +356,34 @@
 
         return carry
 
-    lax.fori_loop(0, chips * pieces, sent, 0)
+    def sent_last(j, carry):
+        @pl.when(not_top)
+        def _():
+            up_last(j).wait_send()
+
+        @pl.when(not_bottom)
+        def _():
+            down_last(j).wait_send()
+
+        to_mate(j).wait_send()
+        store_a(j).wait()
+        return carry
+
+    lax.fori_loop(0, last * pieces, sent, 0)
     for chip in range(chips):
         beside(chip).wait_send()
-    for s in range(pieces):
-        to_mate(s).wait_send()
-        store_a(s).wait()
+    lax.fori_loop(0, tail, sent_last, 0)
     store_k.wait()
 
 
 def call(level, chips, factor, x, g, p, m, v, t):
     tokens, width = g.shape
     rows = p.shape[1]
-    pieces = PIECES
+    pieces, tail = PIECES, TAIL
     dma = pltpu.SemaphoreType.DMA
     any_space = pl.BlockSpec(memory_space=pl.ANY)
     return pl.pallas_call(
-        functools.partial(step_kernel, level, chips, factor, pieces),
+        functools.partial(step_kernel, level, chips, factor, pieces, tail),
         out_shape=(
             jax.ShapeDtypeStruct((tokens, width), jnp.bfloat16),
             jax.ShapeDtypeStruct((1, rows, width), jnp.bfloat16),
@@ -336,13 +405,13 @@
             pltpu.VMEM((tokens, width), jnp.float32),
             pltpu.VMEM((tokens, width), jnp.bfloat16),
             pltpu.VMEM((rows, width), jnp.bfloat16),
-            dma((6,)),
+            dma((pieces,)), dma((6,)),
             dma, dma, dma, dma,
-            dma((chips * pieces,)), dma((chips * pieces,)),
-            dma((chips * pieces,)), dma((chips * pieces,)),
+            dma(((chips - 1) * pieces + tail,)), dma(((chips - 1) * pieces + tail,)),
+            dma(((chips - 1) * pieces + tail,)), dma(((chips - 1) * pieces + tail,)),
             dma((chips,)), dma((chips,)),
-            dma((pieces,)), dma((pieces,)),
-            dma((pieces + 1,)),
+            dma((tail,)), dma((tail,)),
+            dma((tail + 1,)),
         ],
         compiler_params=pltpu.CompilerParams(
             collective_id=level, has_side_effects=True, vmem_limit_bytes=48 * 2**20
@@ -354,14 +423,42 @@
     )(x, g, p, m, v, t)
 
 
+def emit_kernel(first, second, first_out, second_out, sem):
+    copies = [
+        pltpu.make_async_copy(first, first_out, sem.at[0]),
+        pltpu.make_async_copy(second, second_out, sem.at[1]),
+    ]
+    for copy in copies:
+        copy.start()
+    for copy in copies:
+        copy.wait()
+
+
+def emit(first, second):
+    any_space = pl.BlockSpec(memory_space=pl.ANY)
+    return pl.pallas_call(
+        emit_kernel,
+        out_shape=(
+            jax.ShapeDtypeStruct(first.shape, first.dtype),
+            jax.ShapeDtypeStruct(second.shape, second.dtype),
+        ),
+        in_specs=[any_space] * 2,
+        out_specs=(any_space, any_space),
+        scratch_shapes=[pltpu.SemaphoreType.DMA((2,))],
+        name="emit",
+    )(first, second)
+
+
 def per_device(activations, key_grads, params, first_moment, second_moment, step_index):
     factor = activations.shape[1] ** (-0.5)
     chips = lax.axis_size("fsdp") // 2
     levels = lax.axis_size("rep").bit_length() - 1
     branches = [functools.partial(call, level, chips, factor) for level in range(levels)]
-    return lax.switch(
-        step_index[0] % levels, branches, activations, key_grads, params, first_moment, second_moment, step_index
+    key_out, averaged = lax.switch(
+        lax.rem(step_index[0], levels), branches,
+        activations, key_grads, params, first_moment, second_moment, step_index,
     )
+    return emit(key_out, averaged)
 
 
 def solution(mesh):

time: 154 us -> 108 us (0.70)
  the two profiles are of different devices: /device:TPU:22 before, /device:TPU:1 now
where the time goes in v2:
time: 108 us
  Pallas kernels  107 us (99%)
  between operations  1.29 us (1%)
    pallas_call x1, Pallas kernels, call(): pl.pallas_call(functools.partial(step_kernel, level, chips, factor, piece...  106 us

profile of v2, /device:TPU:1, one launch (start us, length us, event | category | flops | bytes accessed | tf_op | source)
XLA Modules:
  0.0 108.2 jit_solution(5312263448461513083)
XLA Ops:
  1.3 106.1 %conditional.1 = ((bf16[128,512]{1,0:T(8,128)(2,1)S(1)}, bf16[1,512,512]{2,1,0:T(8,128)(2,1)S(1)})) conditional(s32[]{:T(128)} %bitcast, (bf16[128,8192]{1,0:T(8,128)(2,1)}, bf16[128,512]{1,0:T(8,128)(2,1)}, f32[1,512,512]{2,1,0:T(8,128)}, bf16[1,512,512]{2,1,0:T(8,128)(2,1)}, bf16[1,512,512]{2,1,0:T(8,128)(2,1)}, ...), branch_computations={%region_0.0_spmd, %region_1.0_spmd, %region_2.0_spmd, %region_3.0_... | conditional | flops 2147483648 | bytes 6291464 | solution.py:457
  1.3 106.0 %level_2.1 = (bf16[128,512]{1,0:T(8,128)(2,1)S(1)}, bf16[1,512,512]{2,1,0:T(8,128)(2,1)S(1)}) custom-call(bf16[128,8192]{1,0:T(8,128)(2,1)} %get-tuple-element.72.x, bf16[128,512]{1,0:T(8,128)(2,1)} %get-tuple-element.73.g, f32[1,512,512]{2,1,0:T(8,128)} %get-tuple-element.74.p, bf16[1,512,512]{2,1,0:T(8,128)(2,1)} %get-tuple-element.75.m, ...), custom_call_target="tpu_custom_call" | custom-call | flops 2147483648 | bytes 6291456 | tf_op jit(solution)/shard_map/cond/branch_2_fun/level_2/pallas_call | solution.py:385
  107.3 0.9 emit.1
